TPU v7x, 128 devices: a whole 4x4x4 slice. The times are simulated.
128 devices in a mesh: grp: 4 (over x), patch: 32 (over y, z, core).
Axes of the slice: x: 4, y: 4, z: 4, core: 2. Of those that a mesh axis runs over, the one named last changes fastest.
Arguments:
- strip_latent: bfloat16 [32768, 512], P(('grp', 'patch')), may hold values from -6 to 6
- strip_owner: int32 [32768, 1], P(('grp', 'patch')), may hold values from 0 to 127; in each aligned block of 256 rows (0 to 255, 256 to 511, ...) at most 8 rows name the same one
- strip_node: int32 [32768], P(('grp', 'patch')), may hold values from 0 to 4095
- dec_first: bfloat16 [512, 512], replicated, may hold values from -0.25 to 0.25
- dec_second: bfloat16 [512, 512], replicated, may hold values from -0.25 to 0.25
- grid_feats: bfloat16 [524288, 512], P(('grp', 'patch')), may hold values from -6 to 6
- g2m_target: int32 [524288], P(('grp', 'patch')), may hold values from 0 to 1535, as said below
- enc_first: bfloat16 [512, 512], replicated, may hold values from -0.25 to 0.25
- enc_second: bfloat16 [512, 512], replicated, may hold values from -0.25 to 0.25
- mesh_init: bfloat16 [65536, 512], P(('grp', 'patch')), may hold values from -6 to 6
- mesh_nbrs: int32 [65536, 6], P(('grp', 'patch')), may hold values from 0 to 639
- proc_self: bfloat16 [512, 512], replicated, may hold values from -0.25 to 0.25
- proc_agg: bfloat16 [512, 512], replicated, may hold values from -0.109375 to 0.109375
- proc_out: bfloat16 [512, 512], replicated, may hold values from -0.25 to 0.25
Outputs:
- mesh_out: bfloat16 [65536, 512], P(('grp', 'patch'))
Inputs may be any that keep to these rules, and one draw needn't show every extreme that they name: `strip_owner`: among the rows of one device no owner is named more than 8 times, a bound that some block reaches. `g2m_target`: A value v names mesh node v % 512 of the patch before (v // 512 = 0), the own patch (1) or the patch after (2) in the same group; the first patch of a group never names the one before, the last never the one after.
All inputs are finite; a program needn't handle non-finite values.
Results may differ from a plain program's by a relative error of at most 0.008.
Values may be sent and summed in bfloat16 or wider, within the bound.
A program may use at most 64 MiB of HBM per device.

v0:
```python
import jax
import jax.numpy as jnp
from jax import lax
from jax.sharding import PartitionSpec as P

CAP = 8
NB = 6
H = 64


def from_behind(block, axis, distance):
    devices = range(lax.axis_size(axis))
    route = [(i - distance, i) for i in devices if i - distance in devices]
    return lax.ppermute(block, axis, route)


def with_halo(block, sides, width):
    for axis, dim in sides:
        count = lax.axis_size(axis)
        forward = [(i, i + 1) for i in range(count - 1)]
        backward = [(target, source) for source, target in forward]
        low = lax.ppermute(
            lax.slice_in_dim(block, block.shape[dim] - width, None, axis=dim), axis, forward
        )
        high = lax.ppermute(lax.slice_in_dim(block, 0, width, axis=dim), axis, backward)
        block = jnp.concatenate([low, block, high], axis=dim)
    return block


def two_layer(inputs, first, second):
    hidden = jax.nn.silu(jnp.dot(inputs, first, preferred_element_type=jnp.float32)).astype(
        jnp.bfloat16
    )
    return jnp.dot(hidden, second, preferred_element_type=jnp.float32).astype(jnp.bfloat16)


def per_device(
    strip_latent,
    strip_owner,
    strip_node,
    dec_first,
    dec_second,
    grid_feats,
    g2m_target,
    enc_first,
    enc_second,
    mesh_init,
    mesh_nbrs,
    proc_self,
    proc_agg,
    proc_out,
):
    groups = lax.axis_size("grp")
    patches = lax.axis_size("patch")
    devices = groups * patches
    grid_rows = grid_feats.shape[0]
    mesh_rows = mesh_init.shape[0]
    slots_all = devices * CAP
    boundary = two_layer(strip_latent, dec_first, dec_second)
    owner = strip_owner[:, 0]
    owner_hit = (owner[:, None] == jnp.arange(devices, dtype=jnp.int32)[None, :]).astype(jnp.int32)
    before_count = jnp.cumsum(owner_hit, axis=0) - owner_hit
    slot = jnp.sum(before_count * owner_hit, axis=1)
    position = owner * CAP + slot
    placed = position[:, None] == jnp.arange(slots_all, dtype=jnp.int32)[None, :]
    send_rows = jnp.einsum(
        "rs,rd->sd", placed.astype(jnp.bfloat16), boundary, preferred_element_type=jnp.float32
    ).astype(jnp.bfloat16)
    send_nodes = jnp.sum(jnp.where(placed, (strip_node + 1)[:, None], 0), axis=0) - 1
    recv_rows, recv_nodes = (
        lax.all_to_all(send_rows, ("grp", "patch"), split_axis=0, concat_axis=0, tiled=True),
        lax.all_to_all(send_nodes, ("grp", "patch"), split_axis=0, concat_axis=0, tiled=True),
    )
    node_hit = (recv_nodes[None, :] == jnp.arange(grid_rows, dtype=jnp.int32)[:, None]).astype(
        jnp.bfloat16
    )
    forcing = jnp.dot(node_hit, recv_rows, preferred_element_type=jnp.float32)
    grid_in = (grid_feats.astype(jnp.float32) + forcing).astype(jnp.bfloat16)
    messages = two_layer(grid_in, enc_first, enc_second)
    before_msgs, before_tgt = from_behind((messages, g2m_target), "patch", 1)
    after_msgs, after_tgt = from_behind((messages, g2m_target), "patch", -1)
    keys = jnp.concatenate([before_tgt - 2 * mesh_rows, g2m_target - mesh_rows, after_tgt])
    stacked = jnp.concatenate([before_msgs, messages, after_msgs], axis=0)
    edge_hit = (keys[None, :] == jnp.arange(mesh_rows, dtype=jnp.int32)[:, None]).astype(
        jnp.bfloat16
    )
    mesh_sum = mesh_init.astype(jnp.float32) + jnp.dot(
        edge_hit, stacked, preferred_element_type=jnp.float32
    )
    mesh_lat = mesh_sum.astype(jnp.bfloat16)
    extended = with_halo(mesh_lat, (("patch", 0),), H)
    ext_keys = jnp.arange(mesh_rows + 2 * H, dtype=jnp.int32)
    counts = jnp.zeros((mesh_rows, mesh_rows + 2 * H), jnp.float32)
    for slot_index in range(NB):
        counts = counts + (mesh_nbrs[:, slot_index][:, None] == ext_keys[None, :]).astype(
            jnp.float32
        )
    agg = jnp.dot(counts.astype(jnp.bfloat16), extended, preferred_element_type=jnp.float32).astype(
        jnp.bfloat16
    )
    pre = jnp.dot(mesh_lat, proc_self, preferred_element_type=jnp.float32) + jnp.dot(
        agg, proc_agg, preferred_element_type=jnp.float32
    )
    proc_hidden = jax.nn.silu(pre).astype(jnp.bfloat16)
    update = jnp.dot(proc_hidden, proc_out, preferred_element_type=jnp.float32)
    return (mesh_lat.astype(jnp.float32) + update).astype(jnp.bfloat16)


def solution(mesh):
    in_specs = (
        P(("grp", "patch"), None),
        P(("grp", "patch"), None),
        P(("grp", "patch")),
        P(),
        P(),
        P(("grp", "patch"), None),
        P(("grp", "patch")),
        P(),
        P(),
        P(("grp", "patch"), None),
        P(("grp", "patch"), None),
        P(),
        P(),
        P(),
    )
    out_specs = P(("grp", "patch"), None)
    return jax.shard_map(
        per_device, mesh=mesh, in_specs=in_specs, out_specs=out_specs, check_vma=False
    )
```

profile of v0, /device:TPU:97, one launch (start us, length us, event | category | flops | bytes accessed | tf_op | source)
XLA Modules:
  0.0 141.8 jit_solution(16080382738943999715)
XLA Ops:
  0.0 0.8 copy.21
  1.2 0.9 fusion.46
  3.6 0.7 sub.21
  4.3 10.2 %all-to-all-start = ((s32[128,8,1]{1,2,0:T(1,128)}), s32[128,8,1]{1,2,0:T(1,128)S(1)}, u32[]{:S(2)}, u32[]{:S(2)}) async-start(s32[128,8,1]{1,2,0:T(1,128)} %bitcast.7), calls=%async_computation | async-start | bytes 131072 | tf_op jit(solution)/shard_map/all_to_all | solution.py:72
  14.5 1.4 %fusion.57 = f32[256,512]{1,0:T(8,128)S(1)} fusion(bf16[256,512]{1,0:T(8,128)(2,1)} %param.14, bf16[512,512]{1,0:T(8,128)(2,1)} %param.17), kind=kOutput, calls=%fused_computation.70 | convolution fusion | flops 134217728 | bytes 1310720 | tf_op jit(solution)/shard_map/dot_general | solution.py:31
  15.9 2.8 %fusion.10 = bf16[128,8,512]{2,1,0:T(8,128)(2,1)} fusion(bf16[512,512]{1,0:T(8,128)(2,1)} %param.18, s32[256]{0:T(256)S(1)} %bitcast.48, f32[256,512]{1,0:T(8,128)S(1)} %fusion.57), kind=kOutput, calls=%fused_computation.16 | convolution fusion | flops 404226048 | bytes 2098176 | tf_op jit(solution)/shard_map/rs,rd->sd/dot_general | solution.py:66
  18.6 2.9 %all-to-all-done = s32[128,8,1]{1,2,0:T(1,128)S(1)} async-done(((s32[128,8,1]{1,2,0:T(1,128)}), s32[128,8,1]{1,2,0:T(1,128)S(1)}, u32[]{:S(2)}, u32[]{:S(2)}) %all-to-all-start) | async-done | bytes 4128 | tf_op jit(solution)/shard_map/all_to_all | solution.py:72
  21.5 7.0 %all-to-all-start.1 = ((bf16[128,8,512]{2,1,0:T(8,128)(2,1)}), bf16[128,8,512]{2,1,0:T(8,128)(2,1)S(1)}, u32[]{:S(2)}, u32[]{:S(2)}) async-start(bf16[128,8,512]{2,1,0:T(8,128)(2,1)} %fusion.10), calls=%async_computation.1 | async-start | bytes 2097152 | tf_op jit(solution)/shard_map/all_to_all | solution.py:71
  29.1 0.8 reduce.3
  30.0 14.8 %all-to-all-done.1 = bf16[128,8,512]{2,1,0:T(8,128)(2,1)S(1)} async-done(((bf16[128,8,512]{2,1,0:T(8,128)(2,1)}), bf16[128,8,512]{2,1,0:T(8,128)(2,1)S(1)}, u32[]{:S(2)}, u32[]{:S(2)}) %all-to-all-start.1) | async-done | bytes 1048608 | tf_op jit(solution)/shard_map/all_to_all | solution.py:71
  44.8 10.7 %fusion.9 = f32[4096,512]{1,0:T(8,128)} fusion(bf16[512,512]{1,0:T(8,128)(2,1)S(1)} %copy-done, bf16[4096,512]{1,0:T(8,128)(2,1)} %param.19, s32[1024]{0:T(1024)S(1)} %eq.173, bf16[128,8,512]{2,1,0:T(8,128)(2,1)S(1)} %all-to-all-done.1), kind=kOutput, calls=%fused_computation.14 | convolution fusion | flops 6452936704 | bytes 14159872 | tf_op jit(solution)/shard_map/dot_general | solution.py:31
  55.5 5.9 %convolution_convert_fusion = bf16[4096,512]{1,0:T(8,128)(2,1)S(1)} fusion(bf16[512,512]{1,0:T(8,128)(2,1)S(1)} %copy-done.5, f32[4096,512]{1,0:T(8,128)} %fusion.9), kind=kOutput, calls=%fused_computation.13 | convolution fusion | flops 2160066560 | bytes 13107200 | tf_op jit(solution)/shard_map/dot_general | solution.py:34
  61.4 5.4 %collective-permute-start.2 = (bf16[4096,512]{1,0:T(8,128)(2,1)S(1)}, bf16[4096,512]{1,0:T(8,128)(2,1)S(1)}, u32[]{:S(2)}, u32[]{:S(2)}) collective-permute-start(bf16[4096,512]{1,0:T(8,128)(2,1)S(1)} %convolution_convert_fusion), channel_id=1, source_target_pairs={{0,1},{1,2},{2,3},{3,4},{4,5},{5,6},{6,7},{7,8},{8,9},{9,10},{10,1... | collective-permute-start | bytes 12582920 | tf_op jit(solution)/shard_map/ppermute | solution.py:14
  66.8 1.9 %collective-permute-start.3 = (bf16[4096,512]{1,0:T(8,128)(2,1)S(1)}, bf16[4096,512]{1,0:T(8,128)(2,1)}, u32[]{:S(2)}, u32[]{:S(2)}) collective-permute-start(bf16[4096,512]{1,0:T(8,128)(2,1)S(1)} %convolution_convert_fusion), channel_id=1, source_target_pairs={{1,0},{2,1},{3,2},{4,3},{5,4},{6,5},{7,6},{8,7},{9,8},{10,9},{11,1... | collective-permute-start | bytes 12582920 | tf_op jit(solution)/shard_map/ppermute | solution.py:14
  68.7 5.8 %collective-permute-start = (s32[4096]{0:T(1024)S(1)}, s32[4096]{0:T(1024)S(1)}, u32[]{:S(2)}, u32[]{:S(2)}) collective-permute-start(s32[4096]{0:T(1024)S(1)} %copy-done.3), channel_id=1, source_target_pairs={{0,1},{1,2},{2,3},{3,4},{4,5},{5,6},{6,7},{7,8},{8,9},{9,10},{10,1... | collective-permute-start | bytes 49160 | tf_op jit(solution)/shard_map/ppermute | solution.py:14
  74.5 2.1 %collective-permute-start.1 = (s32[4096]{0:T(1024)S(1)}, s32[4096]{0:T(1024)S(1)}, u32[]{:S(2)}, u32[]{:S(2)}) collective-permute-start(s32[4096]{0:T(1024)S(1)} %copy-done.3), channel_id=1, source_target_pairs={{1,0},{2,1},{3,2},{4,3},{5,4},{6,5},{7,6},{8,7},{9,8},{10,9},{11,1... | collective-permute-start | bytes 49160 | tf_op jit(solution)/shard_map/ppermute | solution.py:14
  76.6 35.8 %collective-permute-done = s32[4096]{0:T(1024)S(1)} collective-permute-done((s32[4096]{0:T(1024)S(1)}, s32[4096]{0:T(1024)S(1)}, u32[]{:S(2)}, u32[]{:S(2)}) %collective-permute-start) | collective-permute-done | bytes 16416 | tf_op jit(solution)/shard_map/ppermute | solution.py:14
  112.4 6.5 %collective-permute-done.1 = s32[4096]{0:T(1024)S(1)} collective-permute-done((s32[4096]{0:T(1024)S(1)}, s32[4096]{0:T(1024)S(1)}, u32[]{:S(2)}, u32[]{:S(2)}) %collective-permute-start.1) | collective-permute-done | bytes 16416 | tf_op jit(solution)/shard_map/ppermute | solution.py:14
  118.9 9.2 %fusion.14 = bf16[512,512]{1,0:T(8,128)(2,1)S(1)} fusion(bf16[4096,512]{1,0:T(8,128)(2,1)} %collective-permute-done.3, bf16[4096,512]{1,0:T(8,128)(2,1)S(1)} %convolution_convert_fusion, bf16[4096,512]{1,0:T(8,128)(2,1)S(1)} %collective-permute-done.2, s32[12288]{0:T(1024)S(1)} %pad_add_fusion, bf16[512,512]{1,0:T(8,128)(2,1)S(1)} %copy-done.6), kind=kOutput, calls=%fused_computation.27 | convolution fusion | flops 6487277568 | bytes 13680640 | tf_op jit(solution)/shard_map/dot_general | solution.py:87
  128.2 1.9 %collective-permute-start.4 = (bf16[64,512]{1,0:T(8,128)(2,1)S(1)}, bf16[64,512]{1,0:T(8,128)(2,1)S(1)}, u32[]{:S(2)}, u32[]{:S(2)}) collective-permute-start(bf16[64,512]{1,0:T(8,128)(2,1)S(1)} %get-tuple-element.5), channel_id=1, source_target_pairs={{0,1},{1,2},{2,3},{3,4},{4,5},{5,6},{6,7},{7,8},{8,9},{9,10},{10,1... | collective-permute-start | bytes 196616 | tf_op jit(solution)/shard_map/ppermute | solution.py:22
  130.1 2.4 %collective-permute-start.5 = (bf16[64,512]{1,0:T(8,128)(2,1)S(1)}, bf16[64,512]{1,0:T(8,128)(2,1)S(1)}, u32[]{:S(2)}, u32[]{:S(2)}) collective-permute-start(bf16[64,512]{1,0:T(8,128)(2,1)S(1)} %get-tuple-element.6), channel_id=1, source_target_pairs={{1,0},{2,1},{3,2},{4,3},{5,4},{6,5},{7,6},{8,7},{9,8},{10,9},{11,1... | collective-permute-start | bytes 196616 | tf_op jit(solution)/shard_map/ppermute | solution.py:25
  133.0 4.8 %collective-permute-done.5 = bf16[64,512]{1,0:T(8,128)(2,1)S(1)} collective-permute-done((bf16[64,512]{1,0:T(8,128)(2,1)S(1)}, bf16[64,512]{1,0:T(8,128)(2,1)S(1)}, u32[]{:S(2)}, u32[]{:S(2)}) %collective-permute-start.5) | collective-permute-done | bytes 65568 | tf_op jit(solution)/shard_map/ppermute | solution.py:25
  137.8 2.7 %multiply_convert_fusion.2 = bf16[512,512]{1,0:T(8,128)(2,1)S(1)} fusion(f32[512,512]{1,0:T(8,128)S(1)} %fusion.58, bf16[512,512]{1,0:T(8,128)(2,1)} %param.26, bf16[64,512]{1,0:T(8,128)(2,1)S(1)} %collective-permute-done.5, bf16[512,512]{1,0:T(8,128)(2,1)S(1)} %fusion.14, bf16[64,512]{1,0:T(8,128)(2,1)S(1)} %collective-permute-done.4, ...), kind=kOutput, calls=%fused_computation.31 | convolution fusion | flops 613679104 | bytes 2764800 | tf_op jit(solution)/shard_map/dot_general | solution.py:101
  140.6 1.2 add_convert_fusion.2
  (36 shorter events, 2.9 us)
Async XLA Ops:
  0.0 44.8 %copy-start = (bf16[512,512]{1,0:T(8,128)(2,1)S(1)}, bf16[512,512]{1,0:T(8,128)(2,1)}, u32[]{:S(2)}) copy-start(bf16[512,512]{1,0:T(8,128)(2,1)} %param.21) | copy-start | bytes 1572868
  4.3 17.2 %all-to-all-start = ((s32[128,8,1]{1,2,0:T(1,128)}), s32[128,8,1]{1,2,0:T(1,128)S(1)}, u32[]{:S(2)}, u32[]{:S(2)}) async-start(s32[128,8,1]{1,2,0:T(1,128)} %bitcast.7), calls=%async_computation | async-start | bytes 131072 | tf_op jit(solution)/shard_map/all_to_all | solution.py:72
  21.5 23.3 %all-to-all-start.1 = ((bf16[128,8,512]{2,1,0:T(8,128)(2,1)}), bf16[128,8,512]{2,1,0:T(8,128)(2,1)S(1)}, u32[]{:S(2)}, u32[]{:S(2)}) async-start(bf16[128,8,512]{2,1,0:T(8,128)(2,1)} %fusion.10), calls=%async_computation.1 | async-start | bytes 2097152 | tf_op jit(solution)/shard_map/all_to_all | solution.py:71
  30.0 25.5 %copy-start.5 = (bf16[512,512]{1,0:T(8,128)(2,1)S(1)}, bf16[512,512]{1,0:T(8,128)(2,1)}, u32[]{:S(2)}) copy-start(bf16[512,512]{1,0:T(8,128)(2,1)} %param.22) | copy-start | bytes 1572868
  55.5 13.3 %copy-start.3 = (s32[4096]{0:T(1024)S(1)}, s32[4096]{0:T(1024)}, u32[]{:S(2)}) copy-start(s32[4096]{0:T(1024)} %param.20) | copy-start | bytes 49156
  55.5 21.1 %copy-start.4 = (s32[512,6]{0,1:T(8,128)S(1)}, s32[512,6]{0,1:T(8,128)}, u32[]{:S(2)}) copy-start(s32[512,6]{0,1:T(8,128)} %param.24) | copy-start | bytes 36868
  55.5 63.5 %copy-start.6 = (bf16[512,512]{1,0:T(8,128)(2,1)S(1)}, bf16[512,512]{1,0:T(8,128)(2,1)}, u32[]{:S(2)}) copy-start(bf16[512,512]{1,0:T(8,128)(2,1)} %param.23) | copy-start | bytes 1572868
  61.4 57.5 %collective-permute-start.2 = (bf16[4096,512]{1,0:T(8,128)(2,1)S(1)}, bf16[4096,512]{1,0:T(8,128)(2,1)S(1)}, u32[]{:S(2)}, u32[]{:S(2)}) collective-permute-start(bf16[4096,512]{1,0:T(8,128)(2,1)S(1)} %convolution_convert_fusion), channel_id=1, source_target_pairs={{0,1},{1,2},{2,3},{3,4},{4,5},{5,6},{6,7},{7,8},{8,9},{9,10},{10,1... | collective-permute-start | bytes 12582920 | tf_op jit(solution)/shard_map/ppermute | solution.py:14
  66.8 52.1 %collective-permute-start.3 = (bf16[4096,512]{1,0:T(8,128)(2,1)S(1)}, bf16[4096,512]{1,0:T(8,128)(2,1)}, u32[]{:S(2)}, u32[]{:S(2)}) collective-permute-start(bf16[4096,512]{1,0:T(8,128)(2,1)S(1)} %convolution_convert_fusion), channel_id=1, source_target_pairs={{1,0},{2,1},{3,2},{4,3},{5,4},{6,5},{7,6},{8,7},{9,8},{10,9},{11,1... | collective-permute-start | bytes 12582920 | tf_op jit(solution)/shard_map/ppermute | solution.py:14
  68.7 43.7 %collective-permute-start = (s32[4096]{0:T(1024)S(1)}, s32[4096]{0:T(1024)S(1)}, u32[]{:S(2)}, u32[]{:S(2)}) collective-permute-start(s32[4096]{0:T(1024)S(1)} %copy-done.3), channel_id=1, source_target_pairs={{0,1},{1,2},{2,3},{3,4},{4,5},{5,6},{6,7},{7,8},{8,9},{9,10},{10,1... | collective-permute-start | bytes 49160 | tf_op jit(solution)/shard_map/ppermute | solution.py:14
  74.5 44.4 %collective-permute-start.1 = (s32[4096]{0:T(1024)S(1)}, s32[4096]{0:T(1024)S(1)}, u32[]{:S(2)}, u32[]{:S(2)}) collective-permute-start(s32[4096]{0:T(1024)S(1)} %copy-done.3), channel_id=1, source_target_pairs={{1,0},{2,1},{3,2},{4,3},{5,4},{6,5},{7,6},{8,7},{9,8},{10,9},{11,1... | collective-permute-start | bytes 49160 | tf_op jit(solution)/shard_map/ppermute | solution.py:14
  118.9 13.6 %copy-start.1 = (bf16[512,512]{1,0:T(8,128)(2,1)S(1)}, bf16[512,512]{1,0:T(8,128)(2,1)}, u32[]{:S(2)}) copy-start(bf16[512,512]{1,0:T(8,128)(2,1)} %param.25) | copy-start | bytes 1572868
  128.2 4.8 %collective-permute-start.4 = (bf16[64,512]{1,0:T(8,128)(2,1)S(1)}, bf16[64,512]{1,0:T(8,128)(2,1)S(1)}, u32[]{:S(2)}, u32[]{:S(2)}) collective-permute-start(bf16[64,512]{1,0:T(8,128)(2,1)S(1)} %get-tuple-element.5), channel_id=1, source_target_pairs={{0,1},{1,2},{2,3},{3,4},{4,5},{5,6},{6,7},{7,8},{8,9},{9,10},{10,1... | collective-permute-start | bytes 196616 | tf_op jit(solution)/shard_map/ppermute | solution.py:22
  130.1 7.7 %collective-permute-start.5 = (bf16[64,512]{1,0:T(8,128)(2,1)S(1)}, bf16[64,512]{1,0:T(8,128)(2,1)S(1)}, u32[]{:S(2)}, u32[]{:S(2)}) collective-permute-start(bf16[64,512]{1,0:T(8,128)(2,1)S(1)} %get-tuple-element.6), channel_id=1, source_target_pairs={{1,0},{2,1},{3,2},{4,3},{5,4},{6,5},{7,6},{8,7},{9,8},{10,9},{11,1... | collective-permute-start | bytes 196616 | tf_op jit(solution)/shard_map/ppermute | solution.py:25
  137.8 2.7 %copy-start.2 = (bf16[512,512]{1,0:T(8,128)(2,1)S(1)}, bf16[512,512]{1,0:T(8,128)(2,1)}, u32[]{:S(2)}) copy-start(bf16[512,512]{1,0:T(8,128)(2,1)} %param.27) | copy-start | bytes 1572868
where the time goes:
time: 142 us
  waiting for transfers between devices  64.8 us (46%)
  starting transfers between devices  36.6 us (26%)
  matrix products  34.4 us (24%)
  other arithmetic  3.48 us (2%)
  local copies, waits for them, and re-layouts  2.24 us (2%)
    ppermute x4, waiting for transfers between devices, from_behind(): return lax.ppermute(block, axis, route)  42.3 us
    ppermute x4, starting transfers between devices, from_behind(): return lax.ppermute(block, axis, route)  15.1 us
    all_to_all x1, waiting for transfers between devices, per_device(): lax.all_to_all(send_rows, ('grp', 'patch'), split_axis=0, concat_axis=0,...  14.8 us
    dot_general x2, matrix products, two_layer(): jnp.dot(inputs, first, preferred_element_type=jnp.float32)  12.1 us
    all_to_all x1, starting transfers between devices, per_device(): lax.all_to_all(send_nodes, ('grp', 'patch'), split_axis=0, concat_axis=0,...  10.2 us
    dot_general x1, matrix products, per_device(): jnp.dot(edge_hit, stacked, preferred_element_type=jnp.float32)  9.23 us
    all_to_all x1, starting transfers between devices, per_device(): lax.all_to_all(send_rows, ('grp', 'patch'), split_axis=0, concat_axis=0,...  7 us
    dot_general x1, matrix products, two_layer(): jnp.dot(hidden, second, preferred_element_type=jnp.float32)  5.93 us
  transfers between devices with their start and end apart: 8, of which 5 were waited for; matrix products, arithmetic and copies ran while one was open for 4% of the time, Pallas kernels for 0%

commit v1 on v0

v1 whole, which is shorter than its diff:
```python
import jax
import jax.numpy as jnp
from jax import lax
from jax.experimental import pallas as pl
from jax.experimental.pallas import tpu as pltpu
from jax.sharding import PartitionSpec as P

CAP = 8
NB = 6
H = 64
D = 512
GN = 4096
MN = 512
BR = 256
NDEV = 128
SLOTS = NDEV * CAP
CHUNK = 512
NCHUNK = GN // CHUNK
BLK = 256
MESH = pl.DeviceIdType.MESH
F32 = jnp.float32
BF16 = jnp.bfloat16

ORDER = sorted(
    [
        (dx, dy, dz, dc)
        for dx in range(4)
        for dy in range(4)
        for dz in range(4)
        for dc in range(2)
        if dx or dy or dz or dc
    ],
    key=lambda o: (-sum(min(v, 4 - v) for v in o[:3]), (o[0] + 2 * o[1] + 3 * o[2]) % 4, o),
)


def coords():
    g = lax.axis_index("grp")
    p = lax.axis_index("patch")
    return g, p // 8, (p // 2) % 4, p % 2


def shifted(at, offset):
    x, y, z, c = at
    dx, dy, dz, dc = offset
    xx = (x + dx) % 4 if dx else x
    yy = (y + dy) % 4 if dy else y
    zz = (z + dz) % 4 if dz else z
    cc = 1 - c if dc else c
    return xx, yy * 8 + zz * 2 + cc


def silu(v):
    half = v * 0.5
    return half + half * jnp.tanh(half)


def dot(a, b):
    return jnp.dot(a, b, preferred_element_type=F32)


def iota(shape, dim):
    return lax.broadcasted_iota(jnp.int32, shape, dim)


def onehot(mask):
    return jnp.where(mask, 1.0, 0.0).astype(BF16)


def col_to_row(col):
    n = col.shape[0]
    parts = []
    for b in range(n // 128):
        diag = iota((128, 128), 0) == iota((128, 128), 1)
        parts.append(
            jnp.sum(jnp.where(diag, col[b * 128 : (b + 1) * 128], 0.0), axis=0, keepdims=True)
        )
    return jnp.concatenate(parts, axis=1)


def kernel(
    strip, owner, node, d1, d2, feats, tgt, e1, e2, init, nbrs, ps, pa, po,
    out,
    strip_v, owner_v, node_v, d1_v, d2_v, feats_v, tgt_v, e1_v, e2_v, init_v, nbrs_v, ps_v, pa_v, po_v,
    send, nsend, recv, nrecv, sums, g, uj, hj, eq, tp, delta, xs, xr, hr, lat, c_own, c_halo,
    lsem, fsem, s_row, r_row, s_node, r_node, s_x, r_x, s_h, r_h, bar_x, bar_y, own_sem,
):
    at = coords()
    gi = lax.axis_index("grp")
    pi = lax.axis_index("patch")
    me = gi * 32 + pi

    loads = [
        pltpu.make_async_copy(src, dst, lsem.at[i])
        for i, (src, dst) in enumerate(
            [
                (owner, owner_v), (node, node_v), (strip, strip_v), (d1, d1_v), (d2, d2_v),
                (e1, e1_v), (tgt, tgt_v), (nbrs, nbrs_v), (init, init_v), (e2, e2_v),
                (ps, ps_v), (pa, pa_v), (po, po_v),
            ]
        )
    ]

    def feat_load(c):
        rows = pl.ds(pl.multiple_of(c * CHUNK, CHUNK), CHUNK)
        return pltpu.make_async_copy(feats.at[rows], feats_v.at[rows], fsem.at[c])

    barrier = pltpu.get_barrier_semaphore()
    plane = [(0, 0, dz, dc) for dz in range(4) for dc in range(2) if dz or dc]
    xline = [(dx, 0, 0, 0) for dx in (1, 2, 3)]
    yline = [(0, dy, 0, 0) for dy in (1, 2, 3)]
    for o in plane + xline + yline:
        pl.semaphore_signal(barrier, inc=1, device_id=shifted(at, o), device_id_type=MESH)

    for c in loads[:6]:
        c.start()
    for c in range(NCHUNK):
        feat_load(c).start()
    for c in loads[6:]:
        c.start()

    loads[0].wait()
    loads[1].wait()
    owner_row = col_to_row(owner_v[...].astype(F32)).astype(jnp.int32)
    node_row = jnp.concatenate([node_v[0:1, :], node_v[1:2, :]], axis=1).astype(F32)
    hit = iota((NDEV, BR), 0) == owner_row
    upper = onehot(iota((BR, BR), 0) < iota((BR, BR), 1))
    before = dot(onehot(hit), upper)
    slot_row = jnp.sum(jnp.where(hit, before, 0.0), axis=0, keepdims=True).astype(jnp.int32)
    pos_row = owner_row * CAP + slot_row
    placed = iota((SLOTS, BR), 0) == pos_row
    ncol = jnp.sum(jnp.where(placed, node_row + 1.0, 0.0), axis=1, keepdims=True) - 1.0
    ncol = jnp.broadcast_to(ncol.reshape(NDEV, CAP, 1), (NDEV, CAP, 128))
    pick = iota((NDEV, CAP, 128), 1) == iota((NDEV, CAP, 128), 2)
    nsend[...] = jnp.sum(jnp.where(pick, ncol, 0.0), axis=1, keepdims=True)

    pl.semaphore_wait(barrier, len(plane + xline + yline))
    for o in xline:
        pl.semaphore_signal(bar_x, inc=1, device_id=shifted(at, o), device_id_type=MESH)

    for c in loads[2:6]:
        c.wait()
    hid = silu(dot(strip_v[...], d1_v[...])).astype(BF16)
    bnd = dot(hid, d2_v[...]).astype(BF16)
    rows_out = dot(bnd, e1_v[...]).astype(BF16)
    send[...] = dot(onehot(placed), rows_out).astype(BF16).reshape(NDEV, CAP, D)

    pl.semaphore_wait(bar_x, 3)
    for o in yline:
        pl.semaphore_signal(bar_y, inc=1, device_id=shifted(at, o), device_id_type=MESH)
    pl.semaphore_wait(bar_y, 3)

    for o in ORDER:
        to = shifted(at, o)
        idx = to[0] * 32 + to[1]
        pltpu.make_async_remote_copy(
            src_ref=nsend.at[idx], dst_ref=nrecv.at[me], send_sem=s_node, recv_sem=r_node,
            device_id=to, device_id_type=MESH,
        ).start()
    for o in ORDER:
        to = shifted(at, o)
        idx = to[0] * 32 + to[1]
        pltpu.make_async_remote_copy(
            src_ref=send.at[idx], dst_ref=recv.at[me], send_sem=s_row, recv_sem=r_row,
            device_id=to, device_id_type=MESH,
        ).start()
    own_n = pltpu.make_async_copy(nsend.at[me], nrecv.at[me], own_sem.at[0])
    own_r = pltpu.make_async_copy(send.at[me], recv.at[me], own_sem.at[1])
    own_n.start()
    own_r.start()

    for c in loads[6:]:
        c.wait()
    sums[...] = jnp.zeros_like(sums)

    def encode(c, _):
        feat_load(c).wait()
        rows = pl.ds(pl.multiple_of(c * CHUNK, CHUNK), CHUNK)
        h = silu(dot(feats_v[rows, :], e1_v[...])).astype(BF16)
        t = tgt_v[pl.ds(pl.multiple_of(c * (CHUNK // 128), CHUNK // 128), CHUNK // 128), :]
        t_row = jnp.concatenate([t[i : i + 1, :] for i in range(CHUNK // 128)], axis=1)
        for b in range(3):
            hot = onehot(iota((MN, CHUNK), 0) + b * MN == t_row)
            sums[b * MN : (b + 1) * MN, :] += dot(hot, h)
        return 0

    lax.fori_loop(0, NCHUNK, encode, 0)

    halo_lane = iota((MN, 2 * H), 1)
    halo_name = jnp.where(halo_lane < H, halo_lane, halo_lane + MN)
    own_name = iota((MN, MN), 1) + H
    own_cnt = jnp.zeros((MN, MN), F32)
    halo_cnt = jnp.zeros((MN, 2 * H), F32)
    for k in range(NB):
        e = nbrs_v[:, k : k + 1]
        own_cnt += jnp.where(e == own_name, 1.0, 0.0)
        halo_cnt += jnp.where(e == halo_name, 1.0, 0.0)
    c_own[...] = own_cnt.astype(BF16)
    c_halo[...] = halo_cnt.astype(BF16)

    all_n = pltpu.make_async_remote_copy(
        src_ref=nsend.at[pl.ds(0, NDEV - 1)], dst_ref=nrecv.at[pl.ds(0, NDEV - 1)],
        send_sem=s_node, recv_sem=r_node, device_id=(gi, pi), device_id_type=MESH,
    )
    all_n.wait_send()
    all_n.wait_recv()
    own_n.wait()
    got = jnp.broadcast_to(nrecv[...], (NDEV, CAP, 128))
    node_col = jnp.sum(jnp.where(pick, got, 0.0), axis=2, keepdims=True).reshape(SLOTS, 1)
    nrow = col_to_row(node_col)
    same = node_col == nrow
    eq[...] = onehot(same)
    earlier = iota((SLOTS, SLOTS), 0) < iota((SLOTS, SLOTS), 1)
    dup = jnp.sum(jnp.where(same & earlier, 1.0, 0.0), axis=0, keepdims=True)

    node_int = node_col.astype(jnp.int32)
    g[...] = jnp.zeros_like(g)

    def gather(c, _):
        rows = pl.ds(pl.multiple_of(c * CHUNK, CHUNK), CHUNK)
        hot = onehot(iota((SLOTS, CHUNK), 1) + c * CHUNK == node_int)
        g[...] += dot(hot, feats_v[rows, :])
        return 0

    lax.fori_loop(0, NCHUNK, gather, 0)
    u = dot(g[...].astype(BF16), e1_v[...])
    uj[...] = u
    hj[...] = silu(u)

    hi_hot = onehot(iota((SLOTS, GN // 128), 1) == node_int // 128)
    t_all = tgt_v[...]
    t_hi = dot(hi_hot, (t_all // 64).astype(F32).astype(BF16))
    t_lo = dot(hi_hot, (t_all % 64).astype(F32).astype(BF16))
    t_val = t_hi * 64.0 + t_lo
    lane_pick = iota((SLOTS, 128), 1) == node_int % 128
    t_col = jnp.sum(jnp.where(lane_pick, t_val, 0.0), axis=1, keepdims=True)
    t_row = col_to_row(t_col)
    t_row = jnp.where((dup == 0.0) & (nrow >= 0.0), t_row, -1.0).astype(jnp.int32)
    for b in range(3):
        tp[b * MN : (b + 1) * MN, :] = onehot(iota((MN, SLOTS), 0) + b * MN == t_row)

    all_r = pltpu.make_async_remote_copy(
        src_ref=send.at[pl.ds(0, NDEV - 1)], dst_ref=recv.at[pl.ds(0, NDEV - 1)],
        send_sem=s_row, recv_sem=r_row, device_id=(gi, pi), device_id_type=MESH,
    )
    all_r.wait_send()
    all_r.wait_recv()
    own_r.wait()
    f = dot(eq[...], recv[...].reshape(SLOTS, D))
    delta[...] = (silu(uj[...] + f) - hj[...]).astype(BF16)

    up = (gi, (pi + 1) % 32)
    down = (gi, (pi + 31) % 32)
    copies = []
    for b in range(MN // BLK):
        for side, base, to in ((0, 2 * MN, up), (1, 0, down)):
            rows = slice(base + b * BLK, base + (b + 1) * BLK)
            part = pl.ds(b * BLK, BLK)
            xs[side, part, :] = (sums[rows, :] + dot(tp[rows, :], delta[...])).astype(BF16)
            i = 2 * b + side
            c = pltpu.make_async_remote_copy(
                src_ref=xs.at[side, part], dst_ref=xr.at[side, part],
                send_sem=s_x.at[i], recv_sem=r_x.at[i], device_id=to, device_id_type=MESH,
            )
            c.start()
            copies.append(c)
    sums[MN : 2 * MN, :] += dot(tp[MN : 2 * MN, :], delta[...])

    halo = [
        pltpu.make_async_remote_copy(
            src_ref=lat.at[pl.ds(src, H)], dst_ref=hr.at[pl.ds(dst, H)],
            send_sem=s_h.at[i], recv_sem=r_h.at[i], device_id=to, device_id_type=MESH,
        )
        for i, (src, dst, to) in enumerate(((0, H, down), (MN - H, 0, up)))
    ]
    for b in range(MN // BLK):
        copies[2 * b].wait_recv()
        copies[2 * b + 1].wait_recv()
        part = slice(b * BLK, (b + 1) * BLK)
        total = (
            sums[MN + b * BLK : MN + (b + 1) * BLK, :]
            + xr[0, part, :].astype(F32)
            + xr[1, part, :].astype(F32)
        ).astype(BF16)
        lat[part, :] = (init_v[part, :].astype(F32) + dot(total, e2_v[...])).astype(BF16)
        halo[b].start()

    pre = dot(lat[...], ps_v[...])
    agg = dot(c_own[...], lat[...])
    for c in halo:
        c.wait_recv()
    agg = (agg + dot(c_halo[...], hr[...])).astype(BF16)
    ph = silu(pre + dot(agg, pa_v[...])).astype(BF16)
    out[...] = (lat[...].astype(F32) + dot(ph, po_v[...])).astype(BF16)
    for c in copies + halo:
        c.wait_send()


def per_device(strip, owner, node, d1, d2, feats, tgt, e1, e2, init, nbrs, ps, pa, po):
    any_spec = pl.BlockSpec(memory_space=pl.ANY)
    weight = pltpu.VMEM((D, D), BF16)
    dma = pltpu.SemaphoreType.DMA
    return pl.pallas_call(
        kernel,
        out_shape=jax.ShapeDtypeStruct((MN, D), BF16),
        in_specs=[any_spec] * 14,
        out_specs=pl.BlockSpec(memory_space=pltpu.VMEM),
        scratch_shapes=[
            pltpu.VMEM((BR, D), BF16),
            pltpu.VMEM((BR, 1), jnp.int32),
            pltpu.VMEM((BR // 128, 128), jnp.int32),
            weight,
            weight,
            pltpu.VMEM((GN, D), BF16),
            pltpu.VMEM((GN // 128, 128), jnp.int32),
            weight,
            weight,
            pltpu.VMEM((MN, D), BF16),
            pltpu.VMEM((MN, NB), jnp.int32),
            weight,
            weight,
            weight,
            pltpu.VMEM((NDEV, CAP, D), BF16),
            pltpu.VMEM((NDEV, 1, 128), F32),
            pltpu.VMEM((NDEV, CAP, D), BF16),
            pltpu.VMEM((NDEV, 1, 128), F32),
            pltpu.VMEM((3 * MN, D), F32),
            pltpu.VMEM((SLOTS, D), F32),
            pltpu.VMEM((SLOTS, D), F32),
            pltpu.VMEM((SLOTS, D), F32),
            pltpu.VMEM((SLOTS, SLOTS), BF16),
            pltpu.VMEM((3 * MN, SLOTS), BF16),
            pltpu.VMEM((SLOTS, D), BF16),
            pltpu.VMEM((2, MN, D), BF16),
            pltpu.VMEM((2, MN, D), BF16),
            pltpu.VMEM((2 * H, D), BF16),
            pltpu.VMEM((MN, D), BF16),
            pltpu.VMEM((MN, MN), BF16),
            pltpu.VMEM((MN, 2 * H), BF16),
            dma((13,)),
            dma((NCHUNK,)),
            dma,
            dma,
            dma,
            dma,
            dma((2 * MN // BLK,)),
            dma((2 * MN // BLK,)),
            dma((2,)),
            dma((2,)),
            pltpu.SemaphoreType.REGULAR,
            pltpu.SemaphoreType.REGULAR,
            dma((2,)),
        ],
        compiler_params=pltpu.CompilerParams(
            collective_id=0, has_side_effects=True, vmem_limit_bytes=56 * 1024 * 1024
        ),
        name="fused",
    )(
        strip, owner, node.reshape(BR // 128, 128), d1, d2, feats, tgt.reshape(GN // 128, 128),
        e1, e2, init, nbrs, ps, pa, po,
    )


def solution(mesh):
    rows = P(("grp", "patch"), None)
    flat = P(("grp", "patch"))
    in_specs = (rows, rows, flat, P(), P(), rows, flat, P(), P(), rows, rows, P(), P(), P())
    return jax.shard_map(
        per_device, mesh=mesh, in_specs=in_specs, out_specs=rows, check_vma=False
    )
```

time: 142 us -> 57.3 us (0.40)
  the two profiles are of different devices: /device:TPU:97 before, /device:TPU:0 now
where the time goes in v1:
time: 57.3 us; the launch traced here: 57.1 us
  Pallas kernels  52.1 us (91%)
  local copies, waits for them, and re-layouts  4.91 us (9%)
    pallas_call x1, Pallas kernels, per_device(): pl.pallas_call(kernel, out_shape=jax.ShapeDtypeStruct((MN, D), BF16), in_...  52.1 us
    unnamed x3, local copies, waits for them, and re-layouts  4.91 us

profile of v1, /device:TPU:0, one launch (start us, length us, event | category | flops | bytes accessed | tf_op | source)
XLA Modules:
  0.0 57.1 jit_solution(1756861120960685248)
XLA Ops:
  0.0 1.5 %copy.15.owner = s32[256,1]{1,0:T(8,128)} copy(s32[256,1]{0,1:T(1,128)} %param.15) | data formatting | bytes 2048 | tf_op args[1]
  1.5 1.6 %copy.16.nbrs = s32[512,6]{1,0:T(8,128)} copy(s32[512,6]{0,1:T(8,128)} %param.24) | data formatting | bytes 24576 | tf_op args[10]
  3.0 52.1 %fused.1 = bf16[512,512]{1,0:T(8,128)(2,1)} custom-call(bf16[256,512]{1,0:T(8,128)(2,1)} %strip.1, s32[256,1]{1,0:T(8,128)} %copy.15.owner, s32[2,128]{1,0:T(2,128)} %bitcast.3, bf16[512,512]{1,0:T(8,128)(2,1)} %d1.1, bf16[512,512]{1,0:T(8,128)(2,1)} %d2.1, bf16[4096,512]{1,0:T(8,128)(2,1)} %feats.1, s32[32,128]{1,0:T(8,128)} %bitcast.2, ...), custom_call_target="tpu_custom_call" | custom-call | tf_op jit(solution)/shard_map/fused/pallas_call | solution.py:303
  55.2 1.9 %copy.18 = bf16[512,512]{1,0:T(8,128)(2,1)} copy(bf16[512,512]{1,0:T(8,128)(2,1)} %fused.1) | data formatting | bytes 1048576

commit v2 on v1

--- a/solution.py
+++ b/solution.py
@@ -14,9 +14,11 @@
 BR = 256
 NDEV = 128
 SLOTS = NDEV * CAP
-CHUNK = 512
+CHUNK = 2048
 NCHUNK = GN // CHUNK
-BLK = 256
+HALF = 256
+RUNS = ((0, 0, H), (MN - H, H, H), (H, 2 * H, MN - 2 * H))
+PIECES = ((0, 2 * H), (2 * H, 320), (320, MN))
 MESH = pl.DeviceIdType.MESH
 F32 = jnp.float32
 BF16 = jnp.bfloat16
@@ -82,8 +84,8 @@
     strip, owner, node, d1, d2, feats, tgt, e1, e2, init, nbrs, ps, pa, po,
     out,
     strip_v, owner_v, node_v, d1_v, d2_v, feats_v, tgt_v, e1_v, e2_v, init_v, nbrs_v, ps_v, pa_v, po_v,
-    send, nsend, recv, nrecv, sums, g, uj, hj, eq, tp, delta, xs, xr, hr, lat, c_own, c_halo,
-    lsem, fsem, s_row, r_row, s_node, r_node, s_x, r_x, s_h, r_h, bar_x, bar_y, own_sem,
+    send, nsend, recv, nrecv, sums, uj, hj, eq, tp, delta, xs, xr, hr, lat, c_own, c_halo,
+    lsem, fsem, s_row, r_row, s_node, r_node, s_x, r_x, s_h, r_h, own_sem,
 ):
     at = coords()
     gi = lax.axis_index("grp")
@@ -95,9 +97,9 @@
         for i, (src, dst) in enumerate(
             [
                 (owner, owner_v), (node, node_v), (strip, strip_v), (d1, d1_v), (d2, d2_v),
-                (e1, e1_v), (tgt, tgt_v), (nbrs, nbrs_v), (init, init_v), (e2, e2_v),
-                (ps, ps_v), (pa, pa_v), (po, po_v),
+                (e1, e1_v), (tgt, tgt_v), (nbrs, nbrs_v), (e2, e2_v), (ps, ps_v), (pa, pa_v), (po, po_v),
             ]
+            + [(init.at[pl.ds(src, n)], init_v.at[pl.ds(dst, n)]) for src, dst, n in RUNS]
         )
     ]
 
@@ -105,15 +107,11 @@
         rows = pl.ds(pl.multiple_of(c * CHUNK, CHUNK), CHUNK)
         return pltpu.make_async_copy(feats.at[rows], feats_v.at[rows], fsem.at[c])
 
-    barrier = pltpu.get_barrier_semaphore()
-    plane = [(0, 0, dz, dc) for dz in range(4) for dc in range(2) if dz or dc]
-    xline = [(dx, 0, 0, 0) for dx in (1, 2, 3)]
-    yline = [(0, dy, 0, 0) for dy in (1, 2, 3)]
-    for o in plane + xline + yline:
-        pl.semaphore_signal(barrier, inc=1, device_id=shifted(at, o), device_id_type=MESH)
-
     for c in loads[:6]:
         c.start()
+    barrier = pltpu.get_barrier_semaphore()
+    for o in ORDER:
+        pl.semaphore_signal(barrier, inc=1, device_id=shifted(at, o), device_id_type=MESH)
     for c in range(NCHUNK):
         feat_load(c).start()
     for c in loads[6:]:
@@ -121,7 +119,7 @@
 
     loads[0].wait()
     loads[1].wait()
-    owner_row = col_to_row(owner_v[...].astype(F32)).astype(jnp.int32)
+    owner_row = owner_v[...]
     node_row = jnp.concatenate([node_v[0:1, :], node_v[1:2, :]], axis=1).astype(F32)
     hit = iota((NDEV, BR), 0) == owner_row
     upper = onehot(iota((BR, BR), 0) < iota((BR, BR), 1))
@@ -134,10 +132,6 @@
     pick = iota((NDEV, CAP, 128), 1) == iota((NDEV, CAP, 128), 2)
     nsend[...] = jnp.sum(jnp.where(pick, ncol, 0.0), axis=1, keepdims=True)
 
-    pl.semaphore_wait(barrier, len(plane + xline + yline))
-    for o in xline:
-        pl.semaphore_signal(bar_x, inc=1, device_id=shifted(at, o), device_id_type=MESH)
-
     for c in loads[2:6]:
         c.wait()
     hid = silu(dot(strip_v[...], d1_v[...])).astype(BF16)
@@ -145,11 +139,7 @@
     rows_out = dot(bnd, e1_v[...]).astype(BF16)
     send[...] = dot(onehot(placed), rows_out).astype(BF16).reshape(NDEV, CAP, D)
 
-    pl.semaphore_wait(bar_x, 3)
-    for o in yline:
-        pl.semaphore_signal(bar_y, inc=1, device_id=shifted(at, o), device_id_type=MESH)
-    pl.semaphore_wait(bar_y, 3)
-
+    pl.semaphore_wait(barrier, NDEV - 1)
     for o in ORDER:
         to = shifted(at, o)
         idx = to[0] * 32 + to[1]
@@ -171,6 +161,13 @@
 
     for c in loads[6:]:
         c.wait()
+    t_all = tgt_v[...]
+    t_side, t_mesh = t_all // MN, t_all % MN
+    t_mesh = jnp.where(
+        t_mesh < H, t_mesh, jnp.where(t_mesh >= MN - H, t_mesh - (MN - 2 * H), t_mesh + H)
+    )
+    t_all = t_side * MN + t_mesh
+    tgt_v[...] = t_all
     sums[...] = jnp.zeros_like(sums)
 
     def encode(c, _):
@@ -188,11 +185,15 @@
 
     halo_lane = iota((MN, 2 * H), 1)
     halo_name = jnp.where(halo_lane < H, halo_lane, halo_lane + MN)
-    own_name = iota((MN, MN), 1) + H
+    lane = iota((MN, MN), 1)
+    own_name = jnp.where(lane < H, lane + H, jnp.where(lane < 2 * H, lane + MN - H, lane))
     own_cnt = jnp.zeros((MN, MN), F32)
     halo_cnt = jnp.zeros((MN, 2 * H), F32)
+    names = jnp.concatenate([nbrs_v[...].astype(F32), jnp.zeros((8 - NB, MN), F32)], axis=0)
+    names = names.T.astype(jnp.int32)
+    names = jnp.concatenate([names[src : src + n] for src, _, n in RUNS], axis=0)
     for k in range(NB):
-        e = nbrs_v[:, k : k + 1]
+        e = names[:, k : k + 1]
         own_cnt += jnp.where(e == own_name, 1.0, 0.0)
         halo_cnt += jnp.where(e == halo_name, 1.0, 0.0)
     c_own[...] = own_cnt.astype(BF16)
@@ -214,21 +215,15 @@
     dup = jnp.sum(jnp.where(same & earlier, 1.0, 0.0), axis=0, keepdims=True)
 
     node_int = node_col.astype(jnp.int32)
-    g[...] = jnp.zeros_like(g)
-
-    def gather(c, _):
-        rows = pl.ds(pl.multiple_of(c * CHUNK, CHUNK), CHUNK)
+    picked = jnp.zeros((SLOTS, D), F32)
+    for c in range(NCHUNK):
         hot = onehot(iota((SLOTS, CHUNK), 1) + c * CHUNK == node_int)
-        g[...] += dot(hot, feats_v[rows, :])
-        return 0
-
-    lax.fori_loop(0, NCHUNK, gather, 0)
-    u = dot(g[...].astype(BF16), e1_v[...])
+        picked = picked + dot(hot, feats_v[c * CHUNK : (c + 1) * CHUNK, :])
+    u = dot(picked.astype(BF16), e1_v[...])
     uj[...] = u
     hj[...] = silu(u)
 
     hi_hot = onehot(iota((SLOTS, GN // 128), 1) == node_int // 128)
-    t_all = tgt_v[...]
     t_hi = dot(hi_hot, (t_all // 64).astype(F32).astype(BF16))
     t_lo = dot(hi_hot, (t_all % 64).astype(F32).astype(BF16))
     t_val = t_hi * 64.0 + t_lo
@@ -246,24 +241,33 @@
     all_r.wait_send()
     all_r.wait_recv()
     own_r.wait()
-    f = dot(eq[...], recv[...].reshape(SLOTS, D))
-    delta[...] = (silu(uj[...] + f) - hj[...]).astype(BF16)
-
     up = (gi, (pi + 1) % 32)
     down = (gi, (pi + 31) % 32)
-    copies = []
-    for b in range(MN // BLK):
+    copies = {}
+
+    def send_sums(w, b):
+        cols = slice(w * HALF, (w + 1) * HALF)
+        lo, hi = PIECES[b]
+        part = pl.ds(lo, hi - lo)
         for side, base, to in ((0, 2 * MN, up), (1, 0, down)):
-            rows = slice(base + b * BLK, base + (b + 1) * BLK)
-            part = pl.ds(b * BLK, BLK)
-            xs[side, part, :] = (sums[rows, :] + dot(tp[rows, :], delta[...])).astype(BF16)
-            i = 2 * b + side
+            rows = slice(base + lo, base + hi)
+            xs[side, w, part, :] = (sums[rows, cols] + dot(tp[rows, :], delta[:, cols])).astype(BF16)
+            i = (w * len(PIECES) + b) * 2 + side
             c = pltpu.make_async_remote_copy(
-                src_ref=xs.at[side, part], dst_ref=xr.at[side, part],
+                src_ref=xs.at[side, w, part], dst_ref=xr.at[side, w, part],
                 send_sem=s_x.at[i], recv_sem=r_x.at[i], device_id=to, device_id_type=MESH,
             )
             c.start()
-            copies.append(c)
+            copies[w, b, side] = c
+
+    for w in range(D // HALF):
+        cols = slice(w * HALF, (w + 1) * HALF)
+        f = dot(eq[...], recv[:, :, cols].reshape(SLOTS, HALF))
+        delta[:, cols] = (silu(uj[:, cols] + f) - hj[:, cols]).astype(BF16)
+        send_sums(w, 0)
+    for b in range(1, len(PIECES)):
+        for w in range(D // HALF):
+            send_sums(w, b)
     sums[MN : 2 * MN, :] += dot(tp[MN : 2 * MN, :], delta[...])
 
     halo = [
@@ -271,28 +275,39 @@
             src_ref=lat.at[pl.ds(src, H)], dst_ref=hr.at[pl.ds(dst, H)],
             send_sem=s_h.at[i], recv_sem=r_h.at[i], device_id=to, device_id_type=MESH,
         )
-        for i, (src, dst, to) in enumerate(((0, H, down), (MN - H, 0, up)))
+        for i, (src, dst, to) in enumerate(((0, H, down), (H, 0, up)))
     ]
-    for b in range(MN // BLK):
-        copies[2 * b].wait_recv()
-        copies[2 * b + 1].wait_recv()
-        part = slice(b * BLK, (b + 1) * BLK)
-        total = (
-            sums[MN + b * BLK : MN + (b + 1) * BLK, :]
-            + xr[0, part, :].astype(F32)
-            + xr[1, part, :].astype(F32)
+    agg = jnp.zeros((MN, D), F32)
+    pre = []
+    for b, (lo, hi) in enumerate(PIECES):
+        for w in range(D // HALF):
+            for side in range(2):
+                copies[w, b, side].wait_recv()
+        total = [
+            (
+                sums[MN + lo : MN + hi, w * HALF : (w + 1) * HALF]
+                + xr[0, w, lo:hi, :].astype(F32)
+                + xr[1, w, lo:hi, :].astype(F32)
+            ).astype(BF16)
+            for w in range(D // HALF)
+        ]
+        now = (
+            init_v[lo:hi, :].astype(F32) + dot(jnp.concatenate(total, axis=1), e2_v[...])
         ).astype(BF16)
-        lat[part, :] = (init_v[part, :].astype(F32) + dot(total, e2_v[...])).astype(BF16)
-        halo[b].start()
-
-    pre = dot(lat[...], ps_v[...])
-    agg = dot(c_own[...], lat[...])
+        lat[lo:hi, :] = now
+        if b == 0:
+            for c in halo:
+                c.start()
+        pre.append(dot(now, ps_v[...]))
+        agg = agg + dot(c_own[:, lo:hi], now)
     for c in halo:
         c.wait_recv()
     agg = (agg + dot(c_halo[...], hr[...])).astype(BF16)
-    ph = silu(pre + dot(agg, pa_v[...])).astype(BF16)
-    out[...] = (lat[...].astype(F32) + dot(ph, po_v[...])).astype(BF16)
-    for c in copies + halo:
+    hidden = silu(jnp.concatenate(pre, axis=0) + dot(agg, pa_v[...])).astype(BF16)
+    new = (lat[...].astype(F32) + dot(hidden, po_v[...])).astype(BF16)
+    for src, dst, n in RUNS:
+        out[src : src + n, :] = new[dst : dst + n]
+    for c in list(copies.values()) + halo:
         c.wait_send()
 
 
@@ -302,12 +317,12 @@
     dma = pltpu.SemaphoreType.DMA
     return pl.pallas_call(
         kernel,
-        out_shape=jax.ShapeDtypeStruct((MN, D), BF16),
+        out_shape=pltpu.VMEM((MN, D), BF16),
         in_specs=[any_spec] * 14,
         out_specs=pl.BlockSpec(memory_space=pltpu.VMEM),
         scratch_shapes=[
             pltpu.VMEM((BR, D), BF16),
-            pltpu.VMEM((BR, 1), jnp.int32),
+            pltpu.VMEM((1, BR), jnp.int32),
             pltpu.VMEM((BR // 128, 128), jnp.int32),
             weight,
             weight,
@@ -316,7 +331,7 @@
             weight,
             weight,
             pltpu.VMEM((MN, D), BF16),
-            pltpu.VMEM((MN, NB), jnp.int32),
+            pltpu.VMEM((NB, MN), jnp.int32),
             weight,
             weight,
             weight,
@@ -327,28 +342,25 @@
             pltpu.VMEM((3 * MN, D), F32),
             pltpu.VMEM((SLOTS, D), F32),
             pltpu.VMEM((SLOTS, D), F32),
-            pltpu.VMEM((SLOTS, D), F32),
             pltpu.VMEM((SLOTS, SLOTS), BF16),
             pltpu.VMEM((3 * MN, SLOTS), BF16),
             pltpu.VMEM((SLOTS, D), BF16),
-            pltpu.VMEM((2, MN, D), BF16),
-            pltpu.VMEM((2, MN, D), BF16),
+            pltpu.VMEM((2, D // HALF, MN, HALF), BF16),
+            pltpu.VMEM((2, D // HALF, MN, HALF), BF16),
             pltpu.VMEM((2 * H, D), BF16),
             pltpu.VMEM((MN, D), BF16),
             pltpu.VMEM((MN, MN), BF16),
             pltpu.VMEM((MN, 2 * H), BF16),
-            dma((13,)),
+            dma((15,)),
             dma((NCHUNK,)),
             dma,
             dma,
             dma,
             dma,
-            dma((2 * MN // BLK,)),
-            dma((2 * MN // BLK,)),
+            dma((2 * len(PIECES) * (D // HALF),)),
+            dma((2 * len(PIECES) * (D // HALF),)),
             dma((2,)),
             dma((2,)),
-            pltpu.SemaphoreType.REGULAR,
-            pltpu.SemaphoreType.REGULAR,
             dma((2,)),
         ],
         compiler_params=pltpu.CompilerParams(
@@ -356,8 +368,8 @@
         ),
         name="fused",
     )(
-        strip, owner, node.reshape(BR // 128, 128), d1, d2, feats, tgt.reshape(GN // 128, 128),
-        e1, e2, init, nbrs, ps, pa, po,
+        strip, owner.T, node.reshape(BR // 128, 128), d1, d2, feats, tgt.reshape(GN // 128, 128),
+        e1, e2, init, nbrs.T, ps, pa, po,
     )
 
 

time: 57.3 us -> 42.9 us (0.75)
  Pallas kernels: 52.1 us -> 42 us
  local copies, waits for them, and re-layouts: 4.91 us -> 0.8 us
    pallas_call x1, Pallas kernels: 52.1 us -> 42 us  [per_device(): pl.pallas_call(kernel, out_shape=pltpu.VMEM((MN, D), BF16), in_specs=[any...]
    unnamed x3 -> x1, local copies, waits for them, and re-layouts: 4.91 us -> 0.8 us
where the time goes in v2:
time: 42.9 us; the launch traced here: 42.8 us
  Pallas kernels  42 us (98%)
  local copies, waits for them, and re-layouts  0.8 us (2%)
    pallas_call x1, Pallas kernels, per_device(): pl.pallas_call(kernel, out_shape=pltpu.VMEM((MN, D), BF16), in_specs=[any...  42 us

profile of v2, /device:TPU:0, one launch (start us, length us, event | category | flops | bytes accessed | tf_op | source)
XLA Modules:
  0.0 42.8 jit_solution(12686443052905572017)
XLA Ops:
  0.0 42.0 %fused.1 = bf16[512,512]{1,0:T(8,128)(2,1)S(1)} custom-call(bf16[256,512]{1,0:T(8,128)(2,1)} %strip.1, s32[1,256]{1,0:T(1,128)} %bitcast.6, s32[2,128]{1,0:T(2,128)} %bitcast.7, bf16[512,512]{1,0:T(8,128)(2,1)} %d1.1, bf16[512,512]{1,0:T(8,128)(2,1)} %d2.1, bf16[4096,512]{1,0:T(8,128)(2,1)} %feats.1, s32[32,128]{1,0:T(8,128)} %bitcast.4, ...), custom_call_target="tpu_custom_call" | custom-call | tf_op jit(solution)/shard_map/fused/pallas_call | solution.py:318
  42.0 0.8 %copy.16 = bf16[512,512]{1,0:T(8,128)(2,1)} copy(bf16[512,512]{1,0:T(8,128)(2,1)S(1)} %fused.1) | data formatting | bytes 1048576

commit v3 on v2

--- a/solution.py
+++ b/solution.py
@@ -18,7 +18,7 @@
 NCHUNK = GN // CHUNK
 HALF = 256
 RUNS = ((0, 0, H), (MN - H, H, H), (H, 2 * H, MN - 2 * H))
-PIECES = ((0, 2 * H), (2 * H, 320), (320, MN))
+PIECES = (((0, 2 * H), (2 * H, 320), (320, MN)), ((0, 2 * H), (2 * H, MN)))
 MESH = pl.DeviceIdType.MESH
 F32 = jnp.float32
 BF16 = jnp.bfloat16
@@ -84,7 +84,7 @@
     strip, owner, node, d1, d2, feats, tgt, e1, e2, init, nbrs, ps, pa, po,
     out,
     strip_v, owner_v, node_v, d1_v, d2_v, feats_v, tgt_v, e1_v, e2_v, init_v, nbrs_v, ps_v, pa_v, po_v,
-    send, nsend, recv, nrecv, sums, uj, hj, eq, tp, delta, xs, xr, hr, lat, c_own, c_halo,
+    send, nsend, recv, nrecv, sums, u_all, h_all, uj, hj, eq, tp, delta, xs, xr, hr, lat, c_own, c_halo,
     lsem, fsem, s_row, r_row, s_node, r_node, s_x, r_x, s_h, r_h, own_sem,
 ):
     at = coords()
@@ -168,20 +168,29 @@
     )
     t_all = t_side * MN + t_mesh
     tgt_v[...] = t_all
-    sums[...] = jnp.zeros_like(sums)
-
-    def encode(c, _):
+    sums[:MN, :] = jnp.zeros((MN, D), F32)
+    sums[2 * MN :, :] = jnp.zeros((MN, D), F32)
+
+    def targets(c):
+        first = c * (CHUNK // 128)
+        return jnp.concatenate(
+            [tgt_v[first + i : first + i + 1, :] for i in range(CHUNK // 128)], axis=1
+        )
+
+    def encode(c):
         feat_load(c).wait()
-        rows = pl.ds(pl.multiple_of(c * CHUNK, CHUNK), CHUNK)
-        h = silu(dot(feats_v[rows, :], e1_v[...])).astype(BF16)
-        t = tgt_v[pl.ds(pl.multiple_of(c * (CHUNK // 128), CHUNK // 128), CHUNK // 128), :]
-        t_row = jnp.concatenate([t[i : i + 1, :] for i in range(CHUNK // 128)], axis=1)
-        for b in range(3):
+        rows = slice(c * CHUNK, (c + 1) * CHUNK)
+        u = dot(feats_v[rows, :], e1_v[...])
+        u_all[rows, :] = u.astype(BF16)
+        h = silu(u).astype(BF16)
+        h_all[rows, :] = h
+        t_row = targets(c)
+        for b in (0, 2):
             hot = onehot(iota((MN, CHUNK), 0) + b * MN == t_row)
             sums[b * MN : (b + 1) * MN, :] += dot(hot, h)
-        return 0
-
-    lax.fori_loop(0, NCHUNK, encode, 0)
+
+    for c in range(NCHUNK):
+        encode(c)
 
     halo_lane = iota((MN, 2 * H), 1)
     halo_name = jnp.where(halo_lane < H, halo_lane, halo_lane + MN)
@@ -218,10 +227,9 @@
     picked = jnp.zeros((SLOTS, D), F32)
     for c in range(NCHUNK):
         hot = onehot(iota((SLOTS, CHUNK), 1) + c * CHUNK == node_int)
-        picked = picked + dot(hot, feats_v[c * CHUNK : (c + 1) * CHUNK, :])
-    u = dot(picked.astype(BF16), e1_v[...])
-    uj[...] = u
-    hj[...] = silu(u)
+        picked = picked + dot(hot, u_all[c * CHUNK : (c + 1) * CHUNK, :])
+    uj[...] = picked
+    hj[...] = silu(picked)
 
     hi_hot = onehot(iota((SLOTS, GN // 128), 1) == node_int // 128)
     t_hi = dot(hi_hot, (t_all // 64).astype(F32).astype(BF16))
@@ -241,48 +249,66 @@
     all_r.wait_send()
     all_r.wait_recv()
     own_r.wait()
-    up = (gi, (pi + 1) % 32)
-    down = (gi, (pi + 31) % 32)
+    core = pi % 2
+    peers = ((gi, (pi + 31 + 2 * core) % 32), (gi, pi + 1 - 2 * core))
+    bases = (2 * MN * core, 2 * MN * (1 - core))
     copies = {}
 
-    def send_sums(w, b):
+    def send_sums(way, w, pieces):
         cols = slice(w * HALF, (w + 1) * HALF)
-        lo, hi = PIECES[b]
-        part = pl.ds(lo, hi - lo)
-        for side, base, to in ((0, 2 * MN, up), (1, 0, down)):
-            rows = slice(base + lo, base + hi)
-            xs[side, w, part, :] = (sums[rows, cols] + dot(tp[rows, :], delta[:, cols])).astype(BF16)
-            i = (w * len(PIECES) + b) * 2 + side
+        lo, hi = PIECES[way][pieces[0]][0], PIECES[way][pieces[-1]][1]
+        rows = pl.ds(pl.multiple_of(bases[way] + lo, H), hi - lo)
+        xs[way, w, lo:hi, :] = (sums[rows, cols] + dot(tp[rows, :], delta[:, cols])).astype(BF16)
+        for b in pieces:
+            part = pl.ds(PIECES[way][b][0], PIECES[way][b][1] - PIECES[way][b][0])
+            i = ((way * 2) + w) * 3 + b
             c = pltpu.make_async_remote_copy(
-                src_ref=xs.at[side, w, part], dst_ref=xr.at[side, w, part],
-                send_sem=s_x.at[i], recv_sem=r_x.at[i], device_id=to, device_id_type=MESH,
+                src_ref=xs.at[way, w, part], dst_ref=xr.at[way, w, part],
+                send_sem=s_x.at[i], recv_sem=r_x.at[i],
+                device_id=peers[way], device_id_type=MESH,
             )
             c.start()
-            copies[w, b, side] = c
-
+            copies[way, w, b] = c
+
+    forced = [
+        dot(eq[...], recv[:, :, w * HALF : (w + 1) * HALF].reshape(SLOTS, HALF))
+        for w in range(D // HALF)
+    ]
     for w in range(D // HALF):
         cols = slice(w * HALF, (w + 1) * HALF)
-        f = dot(eq[...], recv[:, :, cols].reshape(SLOTS, HALF))
-        delta[:, cols] = (silu(uj[:, cols] + f) - hj[:, cols]).astype(BF16)
-        send_sums(w, 0)
-    for b in range(1, len(PIECES)):
-        for w in range(D // HALF):
-            send_sums(w, b)
-    sums[MN : 2 * MN, :] += dot(tp[MN : 2 * MN, :], delta[...])
+        delta[:, cols] = (silu(uj[:, cols] + forced[w]) - hj[:, cols]).astype(BF16)
+        send_sums(0, w, (0,))
+    for w in range(D // HALF):
+        send_sums(1, w, (0,))
+    for w in range(D // HALF):
+        send_sums(0, w, (1, 2))
+    for w in range(D // HALF):
+        send_sums(1, w, (1,))
+
+    def own_sums(lo, hi):
+        acc = dot(tp[MN + lo : MN + hi, :], delta[...])
+        for c in range(NCHUNK):
+            hot = onehot(iota((hi - lo, CHUNK), 0) + (MN + lo) == targets(c))
+            acc = acc + dot(hot, h_all[c * CHUNK : (c + 1) * CHUNK, :])
+        sums[MN + lo : MN + hi, :] = acc
+
+    own_sums(0, 2 * H)
 
     halo = [
         pltpu.make_async_remote_copy(
-            src_ref=lat.at[pl.ds(src, H)], dst_ref=hr.at[pl.ds(dst, H)],
-            send_sem=s_h.at[i], recv_sem=r_h.at[i], device_id=to, device_id_type=MESH,
+            src_ref=lat.at[pl.ds(pl.multiple_of(src, H), H)],
+            dst_ref=hr.at[pl.ds(pl.multiple_of(H - src, H), H)],
+            send_sem=s_h.at[i], recv_sem=r_h.at[i], device_id=peers[i], device_id_type=MESH,
         )
-        for i, (src, dst, to) in enumerate(((0, H, down), (H, 0, up)))
+        for i, src in enumerate((H * core, H * (1 - core)))
     ]
-    agg = jnp.zeros((MN, D), F32)
-    pre = []
-    for b, (lo, hi) in enumerate(PIECES):
+    pre = jnp.zeros((MN, D), F32)
+    parts = []
+    for b, (lo, hi) in enumerate(PIECES[0]):
         for w in range(D // HALF):
-            for side in range(2):
-                copies[w, b, side].wait_recv()
+            for way in range(2):
+                if b < len(PIECES[way]):
+                    copies[way, w, b].wait_recv()
         total = [
             (
                 sums[MN + lo : MN + hi, w * HALF : (w + 1) * HALF]
@@ -298,12 +324,14 @@
         if b == 0:
             for c in halo:
                 c.start()
-        pre.append(dot(now, ps_v[...]))
-        agg = agg + dot(c_own[:, lo:hi], now)
+            own_sums(2 * H, MN)
+        parts.append(dot(now, ps_v[...]))
+        pre = pre + dot(c_own[:, lo:hi], dot(now, pa_v[...]).astype(BF16))
+    pre = pre + jnp.concatenate(parts, axis=0)
     for c in halo:
         c.wait_recv()
-    agg = (agg + dot(c_halo[...], hr[...])).astype(BF16)
-    hidden = silu(jnp.concatenate(pre, axis=0) + dot(agg, pa_v[...])).astype(BF16)
+    pre = pre + dot(c_halo[...], dot(hr[...], pa_v[...]).astype(BF16))
+    hidden = silu(pre).astype(BF16)
     new = (lat[...].astype(F32) + dot(hidden, po_v[...])).astype(BF16)
     for src, dst, n in RUNS:
         out[src : src + n, :] = new[dst : dst + n]
@@ -340,6 +368,8 @@
             pltpu.VMEM((NDEV, CAP, D), BF16),
             pltpu.VMEM((NDEV, 1, 128), F32),
             pltpu.VMEM((3 * MN, D), F32),
+            pltpu.VMEM((GN, D), BF16),
+            pltpu.VMEM((GN, D), BF16),
             pltpu.VMEM((SLOTS, D), F32),
             pltpu.VMEM((SLOTS, D), F32),
             pltpu.VMEM((SLOTS, SLOTS), BF16),
@@ -357,8 +387,8 @@
             dma,
             dma,
             dma,
-            dma((2 * len(PIECES) * (D // HALF),)),
-            dma((2 * len(PIECES) * (D // HALF),)),
+            dma((12,)),
+            dma((12,)),
             dma((2,)),
             dma((2,)),
             dma((2,)),

time: 42.9 us -> 40.1 us (0.935)
  Pallas kernels: 42 us -> 39.2 us
    pallas_call x1, Pallas kernels: 42 us -> 39.2 us  [per_device(): pl.pallas_call(kernel, out_shape=pltpu.VMEM((MN, D), BF16), in_specs=[any...]
where the time goes in v3:
time: 40.1 us; the launch traced here: 40 us
  Pallas kernels  39.2 us (98%)
  local copies, waits for them, and re-layouts  0.8 us (2%)
    pallas_call x1, Pallas kernels, per_device(): pl.pallas_call(kernel, out_shape=pltpu.VMEM((MN, D), BF16), in_specs=[any...  39.2 us

profile of v3, /device:TPU:0, one launch (start us, length us, event | category | flops | bytes accessed | tf_op | source)
XLA Modules:
  0.0 40.0 jit_solution(6667669985119121539)
XLA Ops:
  0.0 39.2 %fused.1 = bf16[512,512]{1,0:T(8,128)(2,1)S(1)} custom-call(bf16[256,512]{1,0:T(8,128)(2,1)} %strip.1, s32[1,256]{1,0:T(1,128)} %bitcast.6, s32[2,128]{1,0:T(2,128)} %bitcast.7, bf16[512,512]{1,0:T(8,128)(2,1)} %d1.1, bf16[512,512]{1,0:T(8,128)(2,1)} %d2.1, bf16[4096,512]{1,0:T(8,128)(2,1)} %feats.1, s32[32,128]{1,0:T(8,128)} %bitcast.4, ...), custom_call_target="tpu_custom_call" | custom-call | tf_op jit(solution)/shard_map/fused/pallas_call | solution.py:346
  39.2 0.8 %copy.16 = bf16[512,512]{1,0:T(8,128)(2,1)} copy(bf16[512,512]{1,0:T(8,128)(2,1)S(1)} %fused.1) | data formatting | bytes 1048576

commit v4 on v3

--- a/solution.py
+++ b/solution.py
@@ -17,6 +17,7 @@
 CHUNK = 2048
 NCHUNK = GN // CHUNK
 HALF = 256
+FIRST = 96
 RUNS = ((0, 0, H), (MN - H, H, H), (H, 2 * H, MN - 2 * H))
 PIECES = (((0, 2 * H), (2 * H, 320), (320, MN)), ((0, 2 * H), (2 * H, MN)))
 MESH = pl.DeviceIdType.MESH
@@ -84,7 +85,7 @@
     strip, owner, node, d1, d2, feats, tgt, e1, e2, init, nbrs, ps, pa, po,
     out,
     strip_v, owner_v, node_v, d1_v, d2_v, feats_v, tgt_v, e1_v, e2_v, init_v, nbrs_v, ps_v, pa_v, po_v,
-    send, nsend, recv, nrecv, sums, u_all, h_all, uj, hj, eq, tp, delta, xs, xr, hr, lat, c_own, c_halo,
+    send, nsend, recv, nrecv, sums, own, u_all, h_all, uj, hj, eq, tp, delta, xs, xr, hr, lat, c_own, c_halo,
     lsem, fsem, s_row, r_row, s_node, r_node, s_x, r_x, s_h, r_h, own_sem,
 ):
     at = coords()
@@ -140,24 +141,28 @@
     send[...] = dot(onehot(placed), rows_out).astype(BF16).reshape(NDEV, CAP, D)
 
     pl.semaphore_wait(barrier, NDEV - 1)
-    for o in ORDER:
+    for k, o in enumerate(ORDER):
         to = shifted(at, o)
         idx = to[0] * 32 + to[1]
         pltpu.make_async_remote_copy(
-            src_ref=nsend.at[idx], dst_ref=nrecv.at[me], send_sem=s_node, recv_sem=r_node,
+            src_ref=nsend.at[idx], dst_ref=nrecv.at[k], send_sem=s_node, recv_sem=r_node,
             device_id=to, device_id_type=MESH,
         ).start()
-    for o in ORDER:
+    for k, o in enumerate(ORDER):
         to = shifted(at, o)
         idx = to[0] * 32 + to[1]
         pltpu.make_async_remote_copy(
-            src_ref=send.at[idx], dst_ref=recv.at[me], send_sem=s_row, recv_sem=r_row,
-            device_id=to, device_id_type=MESH,
+            src_ref=send.at[idx], dst_ref=recv.at[k], send_sem=s_row,
+            recv_sem=r_row.at[0 if k < FIRST else 1], device_id=to, device_id_type=MESH,
         ).start()
-    own_n = pltpu.make_async_copy(nsend.at[me], nrecv.at[me], own_sem.at[0])
-    own_r = pltpu.make_async_copy(send.at[me], recv.at[me], own_sem.at[1])
+    own_n = pltpu.make_async_copy(nsend.at[me], nrecv.at[NDEV - 1], own_sem.at[0])
+    own_r = pltpu.make_async_copy(send.at[me], recv.at[NDEV - 1], own_sem.at[1])
     own_n.start()
     own_r.start()
+
+    core = pi % 2
+    peers = ((gi, (pi + 31 + 2 * core) % 32), (gi, pi + 1 - 2 * core))
+    bases = (2 * MN * core, 2 * MN * (1 - core))
 
     for c in loads[6:]:
         c.wait()
@@ -168,8 +173,7 @@
     )
     t_all = t_side * MN + t_mesh
     tgt_v[...] = t_all
-    sums[:MN, :] = jnp.zeros((MN, D), F32)
-    sums[2 * MN :, :] = jnp.zeros((MN, D), F32)
+    sums[...] = jnp.zeros_like(sums)
 
     def targets(c):
         first = c * (CHUNK // 128)
@@ -185,9 +189,7 @@
         h = silu(u).astype(BF16)
         h_all[rows, :] = h
         t_row = targets(c)
-        for b in (0, 2):
-            hot = onehot(iota((MN, CHUNK), 0) + b * MN == t_row)
-            sums[b * MN : (b + 1) * MN, :] += dot(hot, h)
+        sums[...] += dot(onehot(iota((MN, CHUNK), 0) + bases[0] == t_row), h)
 
     for c in range(NCHUNK):
         encode(c)
@@ -242,23 +244,37 @@
     for b in range(3):
         tp[b * MN : (b + 1) * MN, :] = onehot(iota((MN, SLOTS), 0) + b * MN == t_row)
 
-    all_r = pltpu.make_async_remote_copy(
-        src_ref=send.at[pl.ds(0, NDEV - 1)], dst_ref=recv.at[pl.ds(0, NDEV - 1)],
-        send_sem=s_row, recv_sem=r_row, device_id=(gi, pi), device_id_type=MESH,
-    )
-    all_r.wait_send()
-    all_r.wait_recv()
+    def arrived(lo, hi, sem):
+        return pltpu.make_async_remote_copy(
+            src_ref=send.at[pl.ds(lo, hi - lo)], dst_ref=recv.at[pl.ds(lo, hi - lo)],
+            send_sem=s_row, recv_sem=sem, device_id=(gi, pi), device_id_type=MESH,
+        )
+
+    def forcing(lo, hi, w):
+        rows = recv[lo:hi, :, w * HALF : (w + 1) * HALF].reshape((hi - lo) * CAP, HALF)
+        return dot(eq[:, lo * CAP : hi * CAP], rows)
+
+    arrived(0, FIRST, r_row.at[0]).wait_recv()
+    forced = [forcing(0, FIRST, w) for w in range(D // HALF)]
+    arrived(0, NDEV - 1, r_row.at[0]).wait_send()
+    arrived(FIRST, NDEV - 1, r_row.at[1]).wait_recv()
     own_r.wait()
-    core = pi % 2
-    peers = ((gi, (pi + 31 + 2 * core) % 32), (gi, pi + 1 - 2 * core))
-    bases = (2 * MN * core, 2 * MN * (1 - core))
+    forced = [forced[w] + forcing(FIRST, NDEV, w) for w in range(D // HALF)]
     copies = {}
+
+    def plain_sums(base, lo, hi):
+        acc = dot(tp[pl.ds(pl.multiple_of(base + lo, H), hi - lo), :], delta[...])
+        for c in range(NCHUNK):
+            hot = onehot(iota((hi - lo, CHUNK), 0) + (base + lo) == targets(c))
+            acc = acc + dot(hot, h_all[c * CHUNK : (c + 1) * CHUNK, :])
+        return acc
 
     def send_sums(way, w, pieces):
         cols = slice(w * HALF, (w + 1) * HALF)
         lo, hi = PIECES[way][pieces[0]][0], PIECES[way][pieces[-1]][1]
-        rows = pl.ds(pl.multiple_of(bases[way] + lo, H), hi - lo)
-        xs[way, w, lo:hi, :] = (sums[rows, cols] + dot(tp[rows, :], delta[:, cols])).astype(BF16)
+        if way == 0:
+            rows = pl.ds(pl.multiple_of(bases[0] + lo, H), hi - lo)
+            xs[0, w, lo:hi, :] = (sums[lo:hi, cols] + dot(tp[rows, :], delta[:, cols])).astype(BF16)
         for b in pieces:
             part = pl.ds(PIECES[way][b][0], PIECES[way][b][1] - PIECES[way][b][0])
             i = ((way * 2) + w) * 3 + b
@@ -270,29 +286,19 @@
             c.start()
             copies[way, w, b] = c
 
-    forced = [
-        dot(eq[...], recv[:, :, w * HALF : (w + 1) * HALF].reshape(SLOTS, HALF))
-        for w in range(D // HALF)
-    ]
     for w in range(D // HALF):
         cols = slice(w * HALF, (w + 1) * HALF)
         delta[:, cols] = (silu(uj[:, cols] + forced[w]) - hj[:, cols]).astype(BF16)
         send_sums(0, w, (0,))
     for w in range(D // HALF):
-        send_sums(1, w, (0,))
-    for w in range(D // HALF):
         send_sums(0, w, (1, 2))
-    for w in range(D // HALF):
-        send_sums(1, w, (1,))
-
-    def own_sums(lo, hi):
-        acc = dot(tp[MN + lo : MN + hi, :], delta[...])
-        for c in range(NCHUNK):
-            hot = onehot(iota((hi - lo, CHUNK), 0) + (MN + lo) == targets(c))
-            acc = acc + dot(hot, h_all[c * CHUNK : (c + 1) * CHUNK, :])
-        sums[MN + lo : MN + hi, :] = acc
-
-    own_sums(0, 2 * H)
+
+    for b, (lo, hi) in enumerate(PIECES[1]):
+        part = plain_sums(bases[1], lo, hi).astype(BF16)
+        for w in range(D // HALF):
+            xs[1, w, lo:hi, :] = part[:, w * HALF : (w + 1) * HALF]
+            send_sums(1, w, (b,))
+    own[: 2 * H, :] = plain_sums(MN, 0, 2 * H)
 
     halo = [
         pltpu.make_async_remote_copy(
@@ -311,7 +317,7 @@
                     copies[way, w, b].wait_recv()
         total = [
             (
-                sums[MN + lo : MN + hi, w * HALF : (w + 1) * HALF]
+                own[lo:hi, w * HALF : (w + 1) * HALF]
                 + xr[0, w, lo:hi, :].astype(F32)
                 + xr[1, w, lo:hi, :].astype(F32)
             ).astype(BF16)
@@ -324,7 +330,7 @@
         if b == 0:
             for c in halo:
                 c.start()
-            own_sums(2 * H, MN)
+            own[2 * H :, :] = plain_sums(MN, 2 * H, MN)
         parts.append(dot(now, ps_v[...]))
         pre = pre + dot(c_own[:, lo:hi], dot(now, pa_v[...]).astype(BF16))
     pre = pre + jnp.concatenate(parts, axis=0)
@@ -367,7 +373,8 @@
             pltpu.VMEM((NDEV, 1, 128), F32),
             pltpu.VMEM((NDEV, CAP, D), BF16),
             pltpu.VMEM((NDEV, 1, 128), F32),
-            pltpu.VMEM((3 * MN, D), F32),
+            pltpu.VMEM((MN, D), F32),
+            pltpu.VMEM((MN, D), F32),
             pltpu.VMEM((GN, D), BF16),
             pltpu.VMEM((GN, D), BF16),
             pltpu.VMEM((SLOTS, D), F32),
@@ -384,7 +391,7 @@
             dma((15,)),
             dma((NCHUNK,)),
             dma,
-            dma,
+            dma((2,)),
             dma,
             dma,
             dma((12,)),

time: 40.1 us -> 38.6 us (0.963)
  Pallas kernels: 39.2 us -> 37.7 us
    pallas_call x1, Pallas kernels: 39.2 us -> 37.7 us  [per_device(): pl.pallas_call(kernel, out_shape=pltpu.VMEM((MN, D), BF16), in_specs=[any...]
where the time goes in v4:
time: 38.6 us; the launch traced here: 38.5 us
  Pallas kernels  37.7 us (98%)
  local copies, waits for them, and re-layouts  0.8 us (2%)
    pallas_call x1, Pallas kernels, per_device(): pl.pallas_call(kernel, out_shape=pltpu.VMEM((MN, D), BF16), in_specs=[any...  37.7 us
    unnamed x1, local copies, waits for them, and re-layouts  0.8 us

profile of v4, /device:TPU:0, one launch (start us, length us, event | category | flops | bytes accessed | tf_op | source)
XLA Modules:
  0.0 38.5 jit_solution(16742625105561792012)
XLA Ops:
  0.0 37.7 %fused.1 = bf16[512,512]{1,0:T(8,128)(2,1)S(1)} custom-call(bf16[256,512]{1,0:T(8,128)(2,1)} %strip.1, s32[1,256]{1,0:T(1,128)} %bitcast.6, s32[2,128]{1,0:T(2,128)} %bitcast.7, bf16[512,512]{1,0:T(8,128)(2,1)} %d1.1, bf16[512,512]{1,0:T(8,128)(2,1)} %d2.1, bf16[4096,512]{1,0:T(8,128)(2,1)} %feats.1, s32[32,128]{1,0:T(8,128)} %bitcast.4, ...), custom_call_target="tpu_custom_call" | custom-call | tf_op jit(solution)/shard_map/fused/pallas_call | solution.py:352
  37.7 0.8 %copy.16 = bf16[512,512]{1,0:T(8,128)(2,1)} copy(bf16[512,512]{1,0:T(8,128)(2,1)S(1)} %fused.1) | data formatting | bytes 1048576

commit v5 on v4

--- a/solution.py
+++ b/solution.py
@@ -294,12 +294,12 @@
         send_sums(0, w, (1, 2))
 
     for b, (lo, hi) in enumerate(PIECES[1]):
+        if b == 1:
+            own[: 2 * H, :] = plain_sums(MN, 0, 2 * H)
         part = plain_sums(bases[1], lo, hi).astype(BF16)
         for w in range(D // HALF):
             xs[1, w, lo:hi, :] = part[:, w * HALF : (w + 1) * HALF]
             send_sums(1, w, (b,))
-    own[: 2 * H, :] = plain_sums(MN, 0, 2 * H)
-
     halo = [
         pltpu.make_async_remote_copy(
             src_ref=lat.at[pl.ds(pl.multiple_of(src, H), H)],

time: 38.6 us -> 38.6 us (level)
  no operation moved by 1% of the time
where the time goes in v5:
time: 38.6 us; the launch traced here: 38.5 us
  Pallas kernels  37.7 us (98%)
  local copies, waits for them, and re-layouts  0.8 us (2%)
    pallas_call x1, Pallas kernels, per_device(): pl.pallas_call(kernel, out_shape=pltpu.VMEM((MN, D), BF16), in_specs=[any...  37.7 us
    unnamed x1, local copies, waits for them, and re-layouts  0.8 us

profile of v5, /device:TPU:0, one launch (start us, length us, event | category | flops | bytes accessed | tf_op | source)
XLA Modules:
  0.0 38.5 jit_solution(8675415559520566438)
XLA Ops:
  0.0 37.7 %fused.1 = bf16[512,512]{1,0:T(8,128)(2,1)S(1)} custom-call(bf16[256,512]{1,0:T(8,128)(2,1)} %strip.1, s32[1,256]{1,0:T(1,128)} %bitcast.6, s32[2,128]{1,0:T(2,128)} %bitcast.7, bf16[512,512]{1,0:T(8,128)(2,1)} %d1.1, bf16[512,512]{1,0:T(8,128)(2,1)} %d2.1, bf16[4096,512]{1,0:T(8,128)(2,1)} %feats.1, s32[32,128]{1,0:T(8,128)} %bitcast.4, ...), custom_call_target="tpu_custom_call" | custom-call | tf_op jit(solution)/shard_map/fused/pallas_call | solution.py:352
  37.7 0.8 %copy.16 = bf16[512,512]{1,0:T(8,128)(2,1)} copy(bf16[512,512]{1,0:T(8,128)(2,1)S(1)} %fused.1) | data formatting | bytes 1048576
